TPU v7x, 256 devices: a whole 4x4x8 slice. The times are simulated.
256 devices in a mesh: dp: 2 (over core), seq: 8 (over x, y_hi), tensor: 16 (over y_lo, z).
Axes of the slice: x: 4, y: 4 (y_hi: 2, y_lo: 2; y = y_hi * 2 + y_lo), z: 8, core: 2. Of those that a mesh axis runs over, the one named last changes fastest.
Arguments:
- hidden: bfloat16 [512, 5376], P(('dp', 'seq')), may hold values from -16 to 16
- weight: bfloat16 [131072, 5376], P(('seq', 'tensor'), 'dp'), may hold values from -6 to 6
- targets: int32 [512], replicated, may hold values from 0 to 131071
- streams: int32 [512], replicated, may hold values from 0 to 7
- loss_token_mask: int32 [512], replicated, may hold values 0 or 1
- counts: int32 [8], replicated, may hold values from 256 to 2047
- stream_weight: float32 [8], replicated, may hold values from 256 to 2048
Outputs:
- grad_hidden: bfloat16 [512, 5376], P(('dp', 'seq'), 'tensor')
- grad_weight: bfloat16 [131072, 5376], P(('seq', 'tensor'), 'dp')
- token_loss: float32 [512], P(('dp', 'seq'))
All inputs are finite; a program needn't handle non-finite values.
Results may differ from a plain program's by a relative error of at most 0.0047.
Values may be sent and summed in bfloat16 or wider, within the bound.
A program may use at most 128 MiB of HBM per device.

v0:
```python
import jax
import jax.numpy as jnp
from jax import lax
from jax.sharding import PartitionSpec as P


def softmax_gradients(logits, vocab_ids, row_targets, row_streams, row_mask, counts, stream_weight):
    target_hit = row_targets[:, None] == vocab_ids
    local_target = jnp.sum(jnp.where(target_hit, logits, 0.0), axis=1)
    row_max = lax.pmax(jnp.max(logits, axis=1), ("seq", "tensor"))
    shifted = jnp.exp(logits - row_max[:, None])
    row_total, target_logit = lax.psum((jnp.sum(shifted, axis=1), local_target), ("seq", "tensor"))
    probabilities = shifted / row_total[:, None]
    stream_fraction = stream_weight / counts.astype(jnp.float32)
    stream_onehot = row_streams[:, None] == lax.broadcasted_iota(
        jnp.int32, (1, stream_fraction.shape[0]), 1
    )
    mask_float = row_mask.astype(jnp.float32)
    token_scale = mask_float * jnp.sum(
        jnp.where(stream_onehot, stream_fraction[None, :], 0.0), axis=1
    )
    cross_entropy = mask_float * (row_max + jnp.log(row_total) - target_logit)
    logit_gradients = (
        token_scale[:, None] * (probabilities - target_hit.astype(jnp.float32))
    ).astype(jnp.bfloat16)
    return (logit_gradients, cross_entropy)


def on_device(hidden, weight, targets, streams, loss_token_mask, counts, stream_weight):
    tok_rows = hidden.shape[0]
    vocab_rows = weight.shape[0]
    half_width = weight.shape[1]
    model_width = 2 * half_width
    sentence_number = lax.axis_size("seq")
    parallel_degree = lax.axis_size("tensor")
    replica = lax.axis_index("dp")
    seq_index = lax.axis_index("seq")
    window = lax.all_gather(hidden, "seq", axis=0, tiled=True)
    win_rows = window.shape[0]
    block_index = seq_index * parallel_degree + lax.axis_index("tensor")
    vocab_ids = block_index * vocab_rows + lax.broadcasted_iota(jnp.int32, (1, vocab_rows), 1)
    full_weight = lax.all_gather(weight, "dp", axis=1, tiled=True)
    logits = lax.dot_general(
        window, full_weight, (((1,), (1,)), ((), ())), preferred_element_type=jnp.float32
    )
    row_start = replica * win_rows
    row_targets = lax.dynamic_slice_in_dim(targets, row_start, win_rows, 0)
    row_streams = lax.dynamic_slice_in_dim(streams, row_start, win_rows, 0)
    row_mask = lax.dynamic_slice_in_dim(loss_token_mask, row_start, win_rows, 0)
    logit_gradients, cross_entropy = softmax_gradients(
        logits, vocab_ids, row_targets, row_streams, row_mask, counts, stream_weight
    )
    token_loss = lax.dynamic_slice_in_dim(cross_entropy, seq_index * tok_rows, tok_rows, 0)
    derivative_pieces = logit_gradients.reshape(sentence_number, tok_rows, vocab_rows)
    coefficient_panels = full_weight.reshape(
        vocab_rows, parallel_degree, model_width // parallel_degree
    )
    hidden_terms = jnp.einsum(
        "vqj,jds->vdqs", derivative_pieces, coefficient_panels, preferred_element_type=jnp.float32
    )
    partial_grad = lax.dot_general(
        logit_gradients, window, (((0,), (0,)), ((), ())), preferred_element_type=jnp.float32
    )
    grad_weight = lax.psum_scatter(partial_grad, "dp", scatter_dimension=1, tiled=True).astype(
        jnp.bfloat16
    )
    hidden_terms = hidden_terms.reshape(
        sentence_number * parallel_degree * tok_rows, model_width // parallel_degree
    )
    grad_hidden = lax.psum_scatter(
        hidden_terms, ("seq", "tensor"), scatter_dimension=0, tiled=True
    ).astype(jnp.bfloat16)
    return (grad_hidden, grad_weight, token_loss)


def solution(mesh):
    in_specs = (P(("dp", "seq"), None), P(("seq", "tensor"), "dp"), P(), P(), P(), P(), P())
    out_specs = (P(("dp", "seq"), "tensor"), P(("seq", "tensor"), "dp"), P(("dp", "seq")))
    return jax.shard_map(
        on_device, mesh=mesh, in_specs=in_specs, out_specs=out_specs, check_vma=False
    )
```

profile of v0, /device:TPU:24, one launch (start us, length us, event | category | flops | bytes accessed | tf_op | source)
XLA Modules:
  0.0 1694.5 jit_solution(7689714243232885733)
XLA Ops:
  7.2 0.0 all-gather.3.cloned.1.call-start
  7.2 0.7 all-gather.3.cloned.1.call-update
  7.9 0.0 all-gather.5.cloned.1.call-start
  7.9 0.7 all-gather.5.cloned.1.call-update
  8.7 0.0 copy-start.1
  8.7 0.0 reduce-scatter.3.cloned.1.call-start
  8.7 0.8 dynamic_slice.14
  9.5 0.8 dynamic_slice.13
  10.2 0.7 convert_divide_fusion
  10.9 0.1 select_reduce_fusion
  11.0 65.7 %all-gather.3.cloned.1.call-done = bf16[256,5376]{1,0:T(8,128)(2,1)} async-done(((bf16[32,5376]{1,0:T(8,128)(2,1)}), bf16[256,5376]{1,0:T(8,128)(2,1)}) %all-gather.3.cloned.1.call-update) | async-done | bytes 2752528 | tf_op jit(solution)/shard_map/all_gather | solution.py:38
  76.7 31.0 %all-gather.5.cloned.1.call-done = bf16[1024,5376]{1,0:T(8,128)(2,1)} async-done(((bf16[1024,2688]{1,0:T(8,128)(2,1)}), bf16[1024,5376]{1,0:T(8,128)(2,1)}) %all-gather.5.cloned.1.call-update) | async-done | bytes 11010064 | tf_op jit(solution)/shard_map/all_gather | solution.py:42
  107.7 6.8 fusion.5
  114.5 291.9 %pmax.7 = f32[256]{0:T(256)S(1)} all-reduce(f32[256]{0:T(256)S(1)} %get-tuple-element.9), channel_id=1, replica_groups=mesh['dp'=2,'seq'=8,'tensor'=16] {'seq','tensor'}, use_global_device_ids=true, to_apply=%region_2.3 | all-reduce | flops 256 | bytes 2048 | tf_op jit(solution)/shard_map/pmax | solution.py:10
  406.4 0.4 fusion.3
  406.8 338.7 %all-reduce = (f32[256]{0:T(256)S(1)}, f32[256]{0:T(256)S(1)}) all-reduce(f32[256]{0:T(256)S(1)} %get-tuple-element.4, f32[256]{0:T(256)S(1)} %get-tuple-element.3), channel_id=1, replica_groups=mesh['dp'=2,'seq'=8,'tensor'=16] {'seq','tensor'}, use_global_device_ids=true, to_apply=%region_4.5 | all-reduce | flops 512 | bytes 4096 | tf_op jit(solution)/shard_map/psum | solution.py:12
  745.5 0.0 copy-done.1
  745.5 0.1 subtract_multiply_fusion
  745.6 0.4 fusion.2
  746.0 14.7 copy.11
  760.7 0.0 copy-start
  760.7 13.2 fusion.6
  773.9 0.0 reduce-scatter.3.cloned.1.call-update
  773.9 0.0 reduce-scatter.5.cloned.1.call-start
  774.0 0.0 copy-done
  774.0 9.0 fusion.7
  783.0 0.0 reduce-scatter.5.cloned.1.call-update
  783.0 0.6 dynamic_slice.15
  783.6 859.0 %reduce-scatter.3.cloned.1.call-done = f32[32,336]{1,0:T(8,128)} async-done(((f32[4096,336]{1,0:T(8,128)}), f32[32,336]{1,0:T(8,128)}) %reduce-scatter.3.cloned.1.call-update) | async-done | bytes 43024 | tf_op jit(solution)/shard_map/reduce_scatter | solution.py:70
  1642.6 1.4 convert_element_type.22
  1644.0 36.8 %reduce-scatter.5.cloned.1.call-done = f32[1024,2688]{1,0:T(8,128)} async-done(((f32[1024,5376]{1,0:T(8,128)}), f32[1024,2688]{1,0:T(8,128)}) %reduce-scatter.5.cloned.1.call-update) | async-done | bytes 11010064 | tf_op jit(solution)/shard_map/reduce_scatter | solution.py:64
  1680.8 7.1 convert_element_type.23
  (1 shorter events, 0.0 us)
Async XLA Ops:
  7.2 69.5 %all-gather.3.cloned.1.call-start = ((), (), s32[]{:S(2)}) async-start(), calls=%async_computation.2 | async-start | bytes 3096576 | tf_op jit(solution)/shard_map/all_gather | solution.py:38
  7.9 99.8 %all-gather.5.cloned.1.call-start = ((), (), s32[]{:S(2)}) async-start(), calls=%async_computation.3 | async-start | bytes 16515072 | tf_op jit(solution)/shard_map/all_gather | solution.py:42
  8.7 736.9 %copy-start.1 = (s32[512]{0:T(512)S(1)}, s32[512]{0:T(512)}, u32[]{:S(2)}) copy-start(s32[512]{0:T(512)} %param.11) | copy-start | bytes 6148
  8.7 1633.9 %reduce-scatter.3.cloned.1.call-start = ((), (), s32[]{:S(2)}) async-start(), calls=%async_computation.4 | async-start | bytes 6340608 | tf_op jit(solution)/shard_map/reduce_scatter | solution.py:70
  760.7 13.3 copy-start
  773.9 906.9 %reduce-scatter.5.cloned.1.call-start = ((), (), s32[]{:S(2)}) async-start(), calls=%async_computation.5 | async-start | bytes 33030144 | tf_op jit(solution)/shard_map/reduce_scatter | solution.py:64
Sparse Core Ops, SparseCore 0:
  10.6 66.0 all-gather.2
  78.5 29.1 all-gather.4
  774.0 868.5 reduce-scatter.2
  1645.2 35.6 reduce-scatter.4
where the time goes:
time: 1700 us; the launch traced here: 1690 us
  waiting for transfers between devices  994 us (58%)
  blocking collectives  631 us (37%)
  matrix products  29 us (2%)
    reduce_scatter x1, waiting for transfers between devices, on_device(): lax.psum_scatter(hidden_terms, ('seq', 'tensor'), scatter_dimension=0, ti...  859 us
    psum x1, blocking collectives, softmax_gradients(): lax.psum((jnp.sum(shifted, axis=1), local_target), ('seq', 'tensor'))  339 us
    pmax x1, blocking collectives, softmax_gradients(): row_max = lax.pmax(jnp.max(logits, axis=1), ('seq', 'tensor'))  292 us
    all_gather x1, waiting for transfers between devices, on_device(): window = lax.all_gather(hidden, 'seq', axis=0, tiled=True)  65.7 us
    reduce_scatter x1, waiting for transfers between devices, on_device(): lax.psum_scatter(partial_grad, 'dp', scatter_dimension=1, tiled=True)  36.8 us
  transfers between devices with their start and end apart: 4, of which 4 were waited for; matrix products, arithmetic and copies ran while one was open for 1% of the time, Pallas kernels for 0%

commit v1 on v0

v1 whole, which is shorter than its diff:
```python
import functools

import jax
import jax.numpy as jnp
from jax import lax
from jax.experimental import pallas as pl
from jax.experimental.pallas import tpu as pltpu
from jax.sharding import PartitionSpec as P

MESH = pl.DeviceIdType.MESH
F32, BF16 = jnp.float32, jnp.bfloat16
V, D, HALF = 1024, 5376, 2688
WA = 1280
WB = HALF - WA
FW = 336
NN = (((1,), (0,)), ((), ()))
NT = (((1,), (1,)), ((), ()))


def device(x, y, z, c):
    return (c, x * 2 + y // 2, (y % 2) * 8 + z)


def aligned(index, unit):
    return pl.multiple_of(index * unit, unit)


def landed(ref, sem):
    pltpu.make_async_copy(ref, ref, sem).wait()


def merge(tiles):
    top = functools.reduce(jnp.maximum, [t[0:1] for t in tiles])
    total = sum(t[1:2] * jnp.exp(t[0:1] - top) for t in tiles)
    target = sum(t[2:3] for t in tiles)
    return top, total, target


def kernel(
    hid, w, tgt, strm, msk, cnt, sw,
    gh, gw, loss,
    wv, hf, part, recv, st_x, st_y, st_z, gt, g, p, gws, lossbuf,
    xa, ya_src, ya, yb, xb_src, xb, fin, zs, zr,
    sem_w, sem_out, sem_send, sem_own, sem_x, sem_f, sem_c, sem_p, sem_l, sem_st, sem_g,
    sem_xa, sem_ya, sem_yb, sem_xb, sem_z,
):
    c, s, t = lax.axis_index("dp"), lax.axis_index("seq"), lax.axis_index("tensor")
    x, yh, yl, z = s // 2, s % 2, t // 8, t % 8
    y = yh * 2 + yl
    sib = device(x, y, z, 1 - c)
    xo = lambda o: (x + o) % 4
    yo = lambda o: (y + o) % 4
    zo = lambda o: (z + o) % 8
    cross, partner = device(x, 3 - y, z, c), device(x, yh * 2 + 1 - yl, z, c)
    sends = []

    def send(src, dst, rsem, dev, unless=None):
        cp = pltpu.make_async_remote_copy(
            src_ref=src, dst_ref=dst, send_sem=sem_send.at[len(sends)], recv_sem=rsem,
            device_id=dev, device_id_type=MESH,
        )
        sends.append((cp, unless))
        if unless is None:
            cp.start()
        else:
            pl.when(jnp.logical_not(unless))(cp.start)

    wcopy = pltpu.make_async_copy(w, wv, sem_w)
    wcopy.start()

    barrier = pltpu.get_barrier_semaphore()
    peers = [sib] + [device(x, y, zo(o), c) for o in range(1, 8)]
    for o in range(1, 4):
        for cc in range(2):
            peers += [device(xo(o), y, z, cc), device(x, yo(o), z, cc)]
    for peer in peers:
        pl.semaphore_signal(barrier, inc=1, device_id=peer, device_id_type=MESH)
    pl.semaphore_wait(barrier, len(peers))

    def blk(k, bx, by, r0=0, n=32):
        return hf.at[k, pl.ds(pl.multiple_of((bx * 2 + by) * 32 + r0, 16), n), :]


    def gather_start(k):
        here = blk(k, x, yh)
        own = pltpu.make_async_copy(hid.at[:, pl.ds(k * HALF, HALF)], here, sem_own.at[k])
        pl.when(c == k)(own.start)
        for o in (1, 3):
            for cc in range(2):
                send(hid.at[:, pl.ds(cc * HALF, HALF)], here, sem_x.at[k, o // 2],
                     device(xo(o), y, z, cc), c != k)
        send(hid.at[:, pl.ds((1 - k) * HALF, HALF)], here, sem_own.at[k], sib, c != k)

    def cross_send(k, j, bx):
        r0 = (1 - yl) * 16
        send(blk(k, bx, yh, r0, 16), blk(k, bx, yh, r0, 16), sem_c.at[k, j], cross)

    def gather_x(k):
        landed(blk(k, x, yh), sem_own.at[k])
        cross_send(k, 0, x)
        landed(blk(k, xo(3), yh), sem_x.at[k, 0])
        send(blk(k, xo(3), yh, 0, 16), blk(k, xo(3), yh, 0, 16), sem_f.at[k, 0],
             device(xo(1), y, z, c))
        landed(blk(k, xo(1), yh), sem_x.at[k, 1])
        send(blk(k, xo(1), yh, 16, 16), blk(k, xo(1), yh, 16, 16), sem_f.at[k, 1],
             device(xo(3), y, z, c))
        cross_send(k, 1, xo(3))
        cross_send(k, 2, xo(1))

    def partner_send(k, j, bx):
        r0 = yl * 16
        ref = blk(k, bx, 1 - yh, r0, 16)
        landed(ref, sem_c.at[k, j])
        send(ref, ref, sem_p.at[k, j], partner)

    def gather_y(k):
        partner_send(k, 0, x)
        landed(blk(k, xo(2), yh, 0, 16), sem_f.at[k, 0])
        landed(blk(k, xo(2), yh, 16, 16), sem_f.at[k, 1])
        cross_send(k, 3, xo(2))
        partner_send(k, 1, xo(3))
        partner_send(k, 2, xo(1))

    def gather_end(k):
        partner_send(k, 3, xo(2))
        r0 = (1 - yl) * 16
        for j, o in enumerate((0, 3, 1, 2)):
            landed(blk(k, xo(o), 1 - yh, r0, 16), sem_p.at[k, j])

    def logits(k):
        def tile(i, _):
            rows = pl.ds(aligned(i, 256), 256)
            full = lax.dot_general(wv[rows, :], hf[k], NT, preferred_element_type=F32)
            part[k, 0, rows, :] = full[:, :128]
            part[k, 1, rows, :] = full[:, 128:]
            return 0

        lax.fori_loop(0, 4, tile, 0)
        send(part.at[k, 1 - c], recv.at[k], sem_l.at[k], sib)

    def row(ref, k):
        return ref[pl.ds(2 * k + c, 1), :]

    def vocab_hit(k, i):
        ids = (s * 16 + t) * V + i * 256 + lax.broadcasted_iota(jnp.int32, (256, 128), 0)
        return ids == row(tgt, k)

    def local_stats(k):
        landed(recv.at[k], sem_l.at[k])

        def add(i, top):
            rows = pl.ds(aligned(i, 256), 256)
            both = part[k, c, rows, :] + recv[k, rows, :]
            recv[k, rows, :] = both
            return jnp.maximum(top, jnp.max(both, axis=0, keepdims=True))

        top = lax.fori_loop(0, 4, add, jnp.full((1, 128), -jnp.inf, F32))

        def expo(i, carry):
            total, target = carry
            rows = pl.ds(aligned(i, 256), 256)
            both = recv[k, rows, :]
            e = jnp.exp(both - top)
            recv[k, rows, :] = e
            target += jnp.sum(jnp.where(vocab_hit(k, i), both, 0.0), axis=0, keepdims=True)
            return total + jnp.sum(e, axis=0, keepdims=True), target

        zero = jnp.zeros((1, 128), F32)
        total, target = lax.fori_loop(0, 4, expo, (zero, zero))
        return top, total, target

    def put(ref, vals):
        ref[...] = jnp.concatenate([*vals, jnp.zeros((5, 128), F32)], axis=0)

    def stats_start(k, buf, vals, me, n, base, dev):
        put(buf.at[k, 0], vals)
        for o in range(1, n):
            send(buf.at[k, 0], buf.at[k, o], sem_st.at[k, base + o], dev(o))

    def stats_end(k, buf, n, base):
        for o in range(1, n):
            landed(buf.at[k, o], sem_st.at[k, base + o])
        return merge([buf[k, o] for o in range(n)])

    def stats_x(k, vals):
        stats_start(k, st_x, vals, x, 4, 0, lambda o: device(xo(o), y, z, c))

    def stats_y(k):
        vals = stats_end(k, st_x, 4, 0)
        stats_start(k, st_y, vals, y, 4, 4, lambda o: device(x, yo(o), z, c))

    def stats_z(k):
        vals = stats_end(k, st_y, 4, 4)
        stats_start(k, st_z, vals, z, 8, 8, lambda o: device(x, y, zo(o), c))

    def grads(k, top0):
        top, total, target = stats_end(k, st_z, 8, 8)
        fraction = jnp.zeros((1, 128), F32)
        for i in range(8):
            weight = jnp.full((1, 128), sw[i], F32)
            count = jnp.full((1, 128), cnt[i], jnp.int32).astype(F32)
            fraction = jnp.where(row(strm, k) == i, weight / count, fraction)
        mask = row(msk, k).astype(F32)
        scale = mask * fraction
        norm = jnp.exp(top0 - top) / total
        lossbuf[k, c] = jnp.broadcast_to(mask * (top + jnp.log(total) - target), (8, 128))
        send(lossbuf.at[k, c], lossbuf.at[k, c], sem_g.at[k, 2], sib)

        cols = pl.ds(aligned(2 * k + c, 128), 128)

        def tile(i, _):
            rows = pl.ds(aligned(i, 256), 256)
            e = recv[k, rows, :]
            hit = jnp.where(vocab_hit(k, i), 1.0, 0.0)
            grad = scale * (e * norm - hit)
            gt[rows, cols] = grad.astype(BF16)
            g[k, pl.ds(aligned(c, 128), 128), rows] = grad.T.astype(BF16)
            return 0

        lax.fori_loop(0, 4, tile, 0)
        mine = pl.ds(aligned(c, 128), 128)
        send(g.at[k, mine], g.at[k, mine], sem_g.at[k, 0], sib)
        send(gt.at[:, cols], gt.at[:, cols], sem_g.at[k, 1], sib)

    def products(k, lo, n):
        def tile(i, _):
            cols = pl.ds(pl.multiple_of(lo + i * 256, 128), 256)
            out = lax.dot_general(g[k], wv[:, cols], NN, preferred_element_type=F32)
            p[k, :, :, :, cols] = out.astype(BF16).reshape(4, 2, 32, 256)
            return 0

        lax.fori_loop(0, n, tile, 0)

    ca, cb = pl.ds(0, WA), pl.ds(WA, WB)

    def to_owner(k, src, dst, sem, h):
        there = h * 2 + c
        own = jnp.logical_and(there == y, c == k)

        pl.when(own)(pltpu.make_async_copy(src, dst, sem).start)
        send(src, dst, sem, device(x, there, z, k), own)

    def hidden_grad(k):
        other = pl.ds(aligned(1 - c, 128), 128)
        landed(g.at[k, other], sem_g.at[k, 0])
        products(k, 0, 5)
        for o in range(1, 4):
            send(p.at[k, xo(o), :, :, ca], xa.at[k, o - 1], sem_xa.at[k, o - 1],
                 device(xo(o), y, z, c))
        products(k, WA, 5)
        tail = pl.ds(HALF - 128, 128)
        out = lax.dot_general(g[k], wv[:, tail], NN, preferred_element_type=F32)
        p[k, :, :, :, tail] = out.astype(BF16).reshape(4, 2, 32, 128)
        for h in range(2):
            to_owner(k, p.at[k, :, h, :, cb], yb.at[y], sem_yb.at[y], h)

    def a_second(k):
        for o in range(3):
            landed(xa.at[k, o], sem_xa.at[k, o])
        for h in range(2):
            total = p[k, x, h, :, 0:WA].astype(F32)
            for o in range(3):
                total += xa[k, o, h].astype(F32)
            ya_src[k, h] = total.astype(BF16)
            to_owner(k, ya_src.at[k, h], ya.at[y], sem_ya.at[y], h)

    def b_second():
        for o in range(4):
            landed(yb.at[o], sem_yb.at[o])
        for bx in range(4):
            total = yb[0, bx].astype(F32)
            for o in range(1, 4):
                total += yb[o, bx].astype(F32)
            xb_src[bx] = total.astype(BF16)
        for o in range(1, 4):
            send(xb_src.at[xo(o)], xb.at[o - 1], sem_xb.at[o - 1], device(xo(o), y, z, c))

    def last():
        for o in range(4):
            landed(ya.at[o], sem_ya.at[o])
        total = ya[0].astype(F32)
        for o in range(1, 4):
            total += ya[o].astype(F32)
        fin[:, 0:WA] = total
        for o in range(3):
            landed(xb.at[o], sem_xb.at[o])
        total = xb_src[x].astype(F32)
        for o in range(3):
            total += xb[o].astype(F32)
        fin[:, WA:HALF] = total
        for i in range(8):
            lo = i * FW // 128 * 128
            wide = min(512, HALF - lo)
            window = fin[:, lo:lo + wide]
            shift = i * FW - lo
            if shift:
                window = pltpu.roll(window, wide - shift, 1)
            zs[i] = window[:, :384].astype(BF16)
        for o in range(1, 8):
            send(zs.at[zo(o)], zr.at[o - 1], sem_z.at[o - 1], device(x, y, zo(o), c))

    def end():
        total = zs[z].astype(F32)
        for o in range(7):
            landed(zr.at[o], sem_z.at[o])
            total += zr[o].astype(F32)
        gh[...] = total[:, :FW].astype(BF16)
        mine = lossbuf[c, x // 2]
        mine = pltpu.roll(mine, (128 - (x % 2) * 64 - yh * 32) % 128, 1)
        loss[...] = mine[0:1, 0:32]

    def head_out(i):
        cols = pl.ds(aligned(i, 256), 256)
        return pltpu.make_async_copy(gws.at[:, cols], gw.at[:, cols], sem_out.at[i])

    def head_grad():
        for k in range(2):
            other = pl.ds(aligned(2 * k + 1 - c, 128), 128)
            landed(gt.at[:, other], sem_g.at[k, 1])
            landed(lossbuf.at[k, 1 - c], sem_g.at[k, 2])

        def tile(i, _):
            cols = pl.ds(aligned(i, 256), 256)
            out = lax.dot_general(gt[:, 0:256], hf[0, :, cols], NN, preferred_element_type=F32)
            out += lax.dot_general(gt[:, 256:512], hf[1, :, cols], NN, preferred_element_type=F32)
            gws[:, cols] = out.astype(BF16)
            head_out(i).start()
            return 0

        lax.fori_loop(0, 10, tile, 0)
        cols = pl.ds(2560, 128)
        out = lax.dot_general(gt[:, 0:256], hf[0, :, cols], NN, preferred_element_type=F32)
        out += lax.dot_general(gt[:, 256:512], hf[1, :, cols], NN, preferred_element_type=F32)
        gws[:, cols] = out.astype(BF16)
        pltpu.make_async_copy(gws.at[:, cols], gw.at[:, cols], sem_out.at[10]).start()

    def head_end():
        def tile(i, _):
            head_out(i).wait()
            return 0

        lax.fori_loop(0, 10, tile, 0)
        cols = pl.ds(2560, 128)
        pltpu.make_async_copy(gws.at[:, cols], gw.at[:, cols], sem_out.at[10]).wait()

    gather_start(0)
    gather_x(0)
    gather_start(1)
    gather_y(0)
    gather_x(1)
    gather_end(0)
    wcopy.wait()
    logits(0)
    gather_y(1)
    vals0 = local_stats(0)
    stats_x(0, vals0)
    gather_end(1)
    logits(1)
    stats_y(0)
    vals1 = local_stats(1)
    stats_x(1, vals1)
    stats_z(0)
    stats_y(1)
    grads(0, vals0[0])
    stats_z(1)
    hidden_grad(0)
    grads(1, vals1[0])
    a_second(0)
    hidden_grad(1)
    a_second(1)
    b_second()
    head_grad()
    last()
    end()
    head_end()
    for cp, unless in sends:
        if unless is None:
            cp.wait_send()
        else:
            pl.when(jnp.logical_not(unless))(cp.wait_send)


def on_device(hidden, weight, targets, streams, loss_token_mask, counts, stream_weight):
    vm = pl.BlockSpec(memory_space=pltpu.VMEM)
    sm = pl.BlockSpec(memory_space=pltpu.SMEM)
    hbm = pl.BlockSpec(memory_space=pl.ANY)
    dma = pltpu.SemaphoreType.DMA
    rows = lambda a: a.reshape(4, 128)
    gh, gw, loss = pl.pallas_call(
        kernel,
        out_shape=(
            jax.ShapeDtypeStruct((32, FW), BF16),
            jax.ShapeDtypeStruct((V, HALF), BF16),
            jax.ShapeDtypeStruct((1, 32), F32),
        ),
        in_specs=[hbm, hbm, vm, vm, vm, sm, sm],
        out_specs=(vm, hbm, vm),
        scratch_shapes=[
            pltpu.VMEM((V, HALF), BF16),
            pltpu.VMEM((2, 256, HALF), BF16),
            pltpu.VMEM((2, 2, V, 128), F32),
            pltpu.VMEM((2, V, 128), F32),
            pltpu.VMEM((2, 4, 8, 128), F32),
            pltpu.VMEM((2, 4, 8, 128), F32),
            pltpu.VMEM((2, 8, 8, 128), F32),
            pltpu.VMEM((V, 512), BF16),
            pltpu.VMEM((2, 256, V), BF16),
            pltpu.VMEM((2, 4, 2, 32, HALF), BF16),
            pltpu.VMEM((V, HALF), BF16),
            pltpu.VMEM((2, 2, 8, 128), F32),
            pltpu.VMEM((2, 3, 2, 32, WA), BF16),
            pltpu.VMEM((2, 2, 32, WA), BF16),
            pltpu.VMEM((4, 32, WA), BF16),
            pltpu.VMEM((4, 4, 32, WB), BF16),
            pltpu.VMEM((4, 32, WB), BF16),
            pltpu.VMEM((3, 32, WB), BF16),
            pltpu.VMEM((32, HALF), F32),
            pltpu.VMEM((8, 32, 384), BF16),
            pltpu.VMEM((7, 32, 384), BF16),
            dma, dma((11,)), dma((128,)), dma((2,)), dma((2, 2)), dma((2, 2)), dma((2, 4)),
            dma((2, 4)), dma((2,)), dma((2, 16)), dma((2, 3)),
            dma((2, 3)), dma((4,)), dma((4,)), dma((3,)), dma((7,)),
        ],
        compiler_params=pltpu.CompilerParams(
            collective_id=0, has_side_effects=True, vmem_limit_bytes=56 << 20
        ),
        name="head",
    )(hidden, weight, rows(targets), rows(streams), rows(loss_token_mask), counts, stream_weight)
    return gh, gw, loss.reshape(32)


def solution(mesh):
    in_specs = (P(("dp", "seq"), None), P(("seq", "tensor"), "dp"), P(), P(), P(), P(), P())
    out_specs = (P(("dp", "seq"), "tensor"), P(("seq", "tensor"), "dp"), P(("dp", "seq")))
    return jax.shard_map(
        on_device, mesh=mesh, in_specs=in_specs, out_specs=out_specs, check_vma=False
    )
```

time: 1700 us -> 98.9 us (0.06)
  waiting for transfers between devices: 994 us -> 0 us
  blocking collectives: 631 us -> 0 us
  Pallas kernels: 0 us -> 89.1 us
  matrix products: 29 us -> 0 us
    reduce_scatter x2 -> x0, waiting for transfers between devices: 896 us -> none  [the longest x1 859 us: on_device(): lax.psum_scatter(hidden_terms, ('seq', 'tensor'), scatter_dimension=0, ti...]
    psum x1 -> x0, blocking collectives: 339 us -> none  [softmax_gradients(): lax.psum((jnp.sum(shifted, axis=1), local_target), ('seq', 'tensor'))]
    pmax x1 -> x0, blocking collectives: 292 us -> none  [softmax_gradients(): row_max = lax.pmax(jnp.max(logits, axis=1), ('seq', 'tensor'))]
    all_gather x2 -> x0, waiting for transfers between devices: 96.7 us -> none  [the longest x1 65.7 us: on_device(): window = lax.all_gather(hidden, 'seq', axis=0, tiled=True)]
    pallas_call x0 -> x1, Pallas kernels: none -> 89.1 us  [on_device(): pl.pallas_call(kernel, out_shape=(jax.ShapeDtypeStruct((32, FW), BF16), j...]
    dot_general x3 -> x0, matrix products: 29 us -> none  [the longest x1 13.2 us: on_device(): jnp.einsum('vqj,jds->vdqs', derivative_pieces, coefficient_panels, prefer...]
  transfers between devices with their start and end apart: 4 -> 0, of which waited for: 4 -> 0; matrix products, arithmetic and copies ran while one was open for 1% -> 0% of each run, Pallas kernels for 0% -> 0%
where the time goes in v1:
time: 98.9 us; the launch traced here: 97 us
  Pallas kernels  89.1 us (90%)
  local copies, waits for them, and re-layouts  7.25 us (7%)
    pallas_call x1, Pallas kernels, on_device(): pl.pallas_call(kernel, out_shape=(jax.ShapeDtypeStruct((32, FW), BF16), j...  89.1 us
    unnamed x5, local copies, waits for them, and re-layouts  7.25 us

profile of v1, /device:TPU:24, one launch (start us, length us, event | category | flops | bytes accessed | tf_op | source)
XLA Modules:
  0.0 97.0 jit_solution(13835097567511971585)
XLA Ops:
  0.6 89.1 %head.1 = (bf16[32,336]{1,0:T(8,128)(2,1)}, bf16[1024,2688]{1,0:T(8,128)(2,1)}, f32[1,32]{1,0:T(1,128)}) custom-call(bf16[32,5376]{1,0:T(8,128)(2,1)} %hid.1, bf16[1024,2688]{1,0:T(8,128)(2,1)} %w.1, s32[4,128]{1,0:T(4,128)} %bitcast.4, s32[4,128]{1,0:T(4,128)} %bitcast.5, s32[4,128]{1,0:T(4,128)} %bitcast.6, s32[8]{0:T(128)} %cnt.1, f32[8]{0:T(128)} %sw.1), custom_call_target="tpu_custom_call" | custom-call | tf_op jit(solution)/shard_map/head/pallas_call | solution.py:389
  89.8 1.3 %copy.13 = bf16[32,336]{1,0:T(8,128)(2,1)} copy(bf16[32,336]{1,0:T(8,128)(2,1)} %get-tuple-element.12) | data formatting | bytes 43008
  91.1 0.0 copy-start
  91.1 5.4 %copy.14 = bf16[1024,2688]{1,0:T(8,128)(2,1)} copy(bf16[1024,2688]{1,0:T(8,128)(2,1)} %get-tuple-element.13) | data formatting | bytes 11010048
  96.5 0.0 copy-done
  96.5 0.5 copy.15
Async XLA Ops:
  91.1 5.4 %copy-start = (f32[1,32]{1,0:T(1,128)S(1)}, f32[1,32]{1,0:T(1,128)}, u32[]{:S(2)}) copy-start(f32[1,32]{1,0:T(1,128)} %get-tuple-element.8) | copy-start | bytes 388

commit v2 on v0

v2 whole, which is shorter than its diff:
```python
import functools

import jax
import jax.numpy as jnp
from jax import lax
from jax.experimental import pallas as pl
from jax.experimental.pallas import tpu as pltpu
from jax.sharding import PartitionSpec as P

MESH = pl.DeviceIdType.MESH
F32, BF16 = jnp.float32, jnp.bfloat16
V, D, HALF = 1024, 5376, 2688
WA = 1280
WB = HALF - WA
FW = 336
NN = (((1,), (0,)), ((), ()))
NT = (((1,), (1,)), ((), ()))


def device(x, y, z, c):
    return (c, x * 2 + y // 2, (y % 2) * 8 + z)


def aligned(index, unit):
    return pl.multiple_of(index * unit, unit)


def landed(ref, sem):
    pltpu.make_async_copy(ref, ref, sem).wait()


def merge(tiles):
    top = functools.reduce(jnp.maximum, [t[0:1] for t in tiles])
    total = sum(t[1:2] * jnp.exp(t[0:1] - top) for t in tiles)
    target = sum(t[2:3] for t in tiles)
    return top, total, target


def kernel(
    hid, w, tgt, strm, msk, cnt, sw,
    gh, gw, loss,
    wv, hf, hs, lg, st_x, st_y, st_z, gt, g, p, lossbuf,
    xa, ya_src, ya, yb, xb_src, xb, fin, zs, zr,
    sem_w, sem_send, sem_own, sem_x, sem_c, sem_p, sem_st, sem_g,
    sem_xa, sem_ya, sem_yb, sem_xb, sem_z,
):
    c, s, t = lax.axis_index("dp"), lax.axis_index("seq"), lax.axis_index("tensor")
    x, yh, yl, z = s // 2, s % 2, t // 8, t % 8
    y = yh * 2 + yl
    sib = device(x, y, z, 1 - c)
    xo = lambda o: (x + o) % 4
    yo = lambda o: (y + o) % 4
    zo = lambda o: (z + o) % 8
    cross = device(x, 3 - y, z, c)
    sends = []

    def send(src, dst, rsem, dev, unless=None):
        cp = pltpu.make_async_remote_copy(
            src_ref=src, dst_ref=dst, send_sem=sem_send.at[len(sends)], recv_sem=rsem,
            device_id=dev, device_id_type=MESH,
        )
        sends.append((cp, unless))
        if unless is None:
            cp.start()
        else:
            pl.when(jnp.logical_not(unless))(cp.start)

    half = z % 2

    def blk(h, bx, by, r0=0, n=32):
        return hf.at[h, pl.ds(pl.multiple_of((bx * 2 + by) * 32 + r0, 16), n), :]

    own = [
        pltpu.make_async_copy(hid.at[:, pl.ds(h * HALF, HALF)], blk(h, x, yh), sem_own.at[h])
        for h in range(2)
    ]
    for cp in own:
        cp.start()
    wcopy = pltpu.make_async_copy(w, wv.at[c], sem_w.at[0])
    wcopy.start()

    barrier = pltpu.get_barrier_semaphore()
    peers = [sib] + [device(x, y, zo(o), c) for o in range(1, 8)]
    for o in range(1, 4):
        peers += [device(xo(o), y, z, c), device(x, yo(o), z, c)]
    for peer in peers:
        pl.semaphore_signal(barrier, inc=1, device_id=peer, device_id_type=MESH)
    pl.semaphore_wait(barrier, len(peers))

    def cross_send(o):
        ref = blk(half, xo(o), yh)
        send(ref, ref, sem_c.at[o], cross)

    def z_send(o, by, base):
        for r in range(2):
            ref = blk(half, xo(o), by, r * 16, 16)
            send(ref, ref, sem_p.at[base + o, r], device(x, y, zo(1 if r == 0 else 7), c))

    def gather_start():
        mine = hid.at[:, pl.ds(aligned(half, HALF), HALF)]
        for o in (1, 3, 2):
            send(mine, blk(half, x, yh), sem_x.at[o - 1], device(xo(o), y, z, c))
        send(mine, blk(half, x, yh), sem_c.at[0], cross)
        send(w, wv.at[c], sem_w.at[1], sib)

    def gather_x(offsets):
        for o in offsets:
            landed(blk(half, xo(o), yh), sem_x.at[3 - o])
            cross_send(o)
            z_send(o, yh, 0)

    def gather_y(offsets):
        for o in offsets:
            landed(blk(half, xo(o), 1 - yh), sem_c.at[o])
            z_send(o, 1 - yh, 4)

    def gather_end():
        for r in range(2):
            for o in range(1, 4):
                landed(blk(1 - half, xo(o), yh, r * 16, 16), sem_p.at[o, r])
            for o in range(4):
                landed(blk(1 - half, xo(o), 1 - yh, r * 16, 16), sem_p.at[4 + o, r])
        for cp in own:
            cp.wait()
        wcopy.wait()
        landed(wv.at[1 - c], sem_w.at[1])

    def logits():
        def tile(i, _):
            rows = pl.ds(aligned(i, 512), 512)
            out = lax.dot_general(wv[0, rows, :], hf[0], NT, preferred_element_type=F32)
            out += lax.dot_general(wv[1, rows, :], hf[1], NT, preferred_element_type=F32)
            lg[rows, :] = out
            return 0

        lax.fori_loop(0, 2, tile, 0)

    def row(ref):
        return jnp.concatenate([ref[pl.ds(2 * c, 1), :], ref[pl.ds(2 * c + 1, 1), :]], axis=1)

    def vocab_hit(i):
        ids = (s * 16 + t) * V + i * 256 + lax.broadcasted_iota(jnp.int32, (256, 256), 0)
        return ids == row(tgt)

    def local_stats():
        def highest(i, top):
            return jnp.maximum(top, jnp.max(lg[pl.ds(aligned(i, 256), 256), :], axis=0, keepdims=True))

        top = lax.fori_loop(0, 4, highest, jnp.full((1, 256), -jnp.inf, F32))

        def expo(i, carry):
            total, target = carry
            rows = pl.ds(aligned(i, 256), 256)
            logit = lg[rows, :]
            e = jnp.exp(logit - top)
            lg[rows, :] = e
            target += jnp.sum(jnp.where(vocab_hit(i), logit, 0.0), axis=0, keepdims=True)
            return total + jnp.sum(e, axis=0, keepdims=True), target

        zero = jnp.zeros((1, 256), F32)
        total, target = lax.fori_loop(0, 4, expo, (zero, zero))
        return top, total, target

    def exchange(buf, vals, n, base, dev):
        buf[0] = jnp.concatenate([*vals, jnp.zeros((5, 256), F32)], axis=0)
        for o in range(1, n):
            send(buf.at[0], buf.at[o], sem_st.at[base + o], dev(o))
        for o in range(1, n):
            landed(buf.at[o], sem_st.at[base + o])
        return merge([buf[o] for o in range(n)])

    def grads():
        vals = local_stats()
        top0 = vals[0]
        vals = exchange(st_x, vals, 4, 0, lambda o: device(xo(o), y, z, c))
        vals = exchange(st_y, vals, 4, 4, lambda o: device(x, yo(o), z, c))
        top, total, target = exchange(st_z, vals, 8, 8, lambda o: device(x, y, zo(o), c))
        fraction = jnp.zeros((1, 256), F32)
        for i in range(8):
            weight = jnp.full((1, 256), sw[i], F32)
            count = jnp.full((1, 256), cnt[i], jnp.int32).astype(F32)
            fraction = jnp.where(row(strm) == i, weight / count, fraction)
        mask = row(msk).astype(F32)
        scale = mask * fraction
        norm = jnp.exp(top0 - top) / total
        row_loss = mask * (top + jnp.log(total) - target)
        for h in range(2):
            lossbuf[h] = jnp.broadcast_to(row_loss[:, h * 128:h * 128 + 128], (8, 128))

        def tile(i, _):
            rows = pl.ds(aligned(i, 256), 256)
            hit = jnp.where(vocab_hit(i), 1.0, 0.0)
            grad = scale * (lg[rows, :] * norm - hit)
            gt[c, rows, :] = grad.astype(BF16)
            g[:, rows] = grad.T.astype(BF16)
            return 0

        lax.fori_loop(0, 4, tile, 0)
        send(gt.at[c], gt.at[c], sem_g.at[0], sib)

    ca, cb = pl.ds(0, WA), pl.ds(WA, WB)

    def products(h, lo, n):
        def tile(i, _):
            cols = pl.ds(pl.multiple_of(lo + i * 256, 128), 256)
            out = lax.dot_general(g[...], wv[h, :, cols], NN, preferred_element_type=F32)
            p[h, :, :, :, cols] = out.astype(BF16).reshape(4, 2, 32, 256)
            return 0

        lax.fori_loop(0, n, tile, 0)

    def a_first(h):
        products(h, 0, 5)
        for o in (2, 1, 3):
            send(p.at[h, xo(o), :, :, ca], xa.at[h, o - 1], sem_xa.at[h, o - 1],
                 device(xo(o), y, z, c))

    def b_first():
        for h in range(2):
            products(h, WA, 5)
            tail = pl.ds(HALF - 128, 128)
            out = lax.dot_general(g[...], wv[h, :, tail], NN, preferred_element_type=F32)
            p[h, :, :, :, tail] = out.astype(BF16).reshape(4, 2, 32, 128)
        for o in (2, 1, 3):
            there = yo(o)
            send(p.at[there % 2, :, there // 2, :, cb], yb.at[o - 1], sem_yb.at[o - 1],
                 device(x, there, z, c))

    def a_second(h):
        for o in range(3):
            landed(xa.at[h, o], sem_xa.at[h, o])
        for k in range(2):
            total = p[h, x, k, :, 0:WA].astype(F32)
            for o in range(3):
                total += xa[h, o, k].astype(F32)
            ya_src[h, k] = total.astype(BF16)
            there = 2 * k + h
            send(ya_src.at[h, k], ya.at[y], sem_ya.at[y], device(x, there, z, c), there == y)

    def b_second():
        for o in range(3):
            landed(yb.at[o], sem_yb.at[o])
        for k in range(4):
            total = p[yl, k, yh, :, WA:HALF].astype(F32)
            for o in range(3):
                total += yb[o, k].astype(F32)
            xb_src[k] = total.astype(BF16)
        for o in (2, 1, 3):
            send(xb_src.at[xo(o)], xb.at[o - 1], sem_xb.at[o - 1], device(xo(o), y, z, c))

    def last():
        total = ya_src[yl, yh].astype(F32)
        for o in range(1, 4):
            landed(ya.at[yo(o)], sem_ya.at[yo(o)])
            total += ya[yo(o)].astype(F32)
        fin[:, 0:WA] = total
        total = xb_src[x].astype(F32)
        for o in range(3):
            landed(xb.at[o], sem_xb.at[o])
            total += xb[o].astype(F32)
        fin[:, WA:HALF] = total
        for i in range(8):
            lo = i * FW // 128 * 128
            wide = min(512, HALF - lo)
            window = fin[:, lo:lo + wide]
            shift = i * FW - lo
            if shift:
                window = pltpu.roll(window, wide - shift, 1)
            zs[i] = window[:, :384].astype(BF16)
        for o in (4, 3, 5, 2, 6, 1, 7):
            send(zs.at[zo(o)], zr.at[o - 1], sem_z.at[o - 1], device(x, y, zo(o), c))

    def end():
        total = zs[z].astype(F32)
        for o in range(7):
            landed(zr.at[o], sem_z.at[o])
            total += zr[o].astype(F32)
        gh[...] = total[:, :FW].astype(BF16)
        row_loss = lossbuf[x // 2]
        row_loss = pltpu.roll(row_loss, (128 - (x % 2) * 64 - yh * 32) % 128, 1)
        loss[...] = row_loss[0:1, 0:32]

    def head_tile(cols):
        out = lax.dot_general(gt[c], hf[c, :, cols], NN, preferred_element_type=F32)
        out += lax.dot_general(gt[1 - c], hs[:, cols], NN, preferred_element_type=F32)
        gw[:, cols] = out.astype(BF16)

    def head_grad():
        landed(gt.at[1 - c], sem_g.at[0])
        landed(hs, sem_g.at[1])

        def tile(i, _):
            head_tile(pl.ds(aligned(i, 256), 256))
            return 0

        lax.fori_loop(0, 10, tile, 0)
        head_tile(pl.ds(2560, 128))

    gather_start()
    gather_x((1, 3))
    gather_y((0,))
    gather_x((2,))
    gather_y((1, 3, 2))
    gather_end()
    logits()
    send(hf.at[1 - c], hs, sem_g.at[1], sib)
    grads()
    a_first(0)
    b_first()
    a_first(1)
    head_grad()
    a_second(0)
    a_second(1)
    b_second()
    last()
    end()
    for cp, unless in sends:
        if unless is None:
            cp.wait_send()
        else:
            pl.when(jnp.logical_not(unless))(cp.wait_send)


def on_device(hidden, weight, targets, streams, loss_token_mask, counts, stream_weight):
    vm = pl.BlockSpec(memory_space=pltpu.VMEM)
    sm = pl.BlockSpec(memory_space=pltpu.SMEM)
    hbm = pl.BlockSpec(memory_space=pl.ANY)
    dma = pltpu.SemaphoreType.DMA
    rows = lambda a: a.reshape(4, 128)
    outs = (((32, FW), BF16), ((V, HALF), BF16), ((1, 32), F32))
    gh, gw, loss = pl.pallas_call(
        kernel,
        out_shape=tuple(pltpu.VMEM(*out) for out in outs),
        in_specs=[hbm, hbm, vm, vm, vm, sm, sm],
        out_specs=(vm, vm, vm),
        scratch_shapes=[
            pltpu.VMEM((2, V, HALF), BF16),
            pltpu.VMEM((2, 256, HALF), BF16),
            pltpu.VMEM((256, HALF), BF16),
            pltpu.VMEM((V, 256), F32),
            pltpu.VMEM((4, 8, 256), F32),
            pltpu.VMEM((4, 8, 256), F32),
            pltpu.VMEM((8, 8, 256), F32),
            pltpu.VMEM((2, V, 256), BF16),
            pltpu.VMEM((256, V), BF16),
            pltpu.VMEM((2, 4, 2, 32, HALF), BF16),
            pltpu.VMEM((2, 8, 128), F32),
            pltpu.VMEM((2, 3, 2, 32, WA), BF16),
            pltpu.VMEM((2, 2, 32, WA), BF16),
            pltpu.VMEM((4, 32, WA), BF16),
            pltpu.VMEM((3, 4, 32, WB), BF16),
            pltpu.VMEM((4, 32, WB), BF16),
            pltpu.VMEM((3, 32, WB), BF16),
            pltpu.VMEM((32, HALF), F32),
            pltpu.VMEM((8, 32, 384), BF16),
            pltpu.VMEM((7, 32, 384), BF16),
            dma((2,)), dma((96,)), dma((2,)), dma((3,)), dma((4,)), dma((8, 2)), dma((16,)),
            dma((2,)),
            dma((2, 3)), dma((4,)), dma((3,)), dma((3,)), dma((7,)),
        ],
        compiler_params=pltpu.CompilerParams(
            collective_id=0, has_side_effects=True, vmem_limit_bytes=56 << 20
        ),
        name="head",
    )(hidden, weight, rows(targets), rows(streams), rows(loss_token_mask), counts, stream_weight)
    return gh, gw, loss.reshape(32)


def solution(mesh):
    in_specs = (P(("dp", "seq"), None), P(("seq", "tensor"), "dp"), P(), P(), P(), P(), P())
    out_specs = (P(("dp", "seq"), "tensor"), P(("seq", "tensor"), "dp"), P(("dp", "seq")))
    return jax.shard_map(
        on_device, mesh=mesh, in_specs=in_specs, out_specs=out_specs, check_vma=False
    )
```

time: 1700 us -> 83.6 us (0.05)
  waiting for transfers between devices: 994 us -> 0 us
  blocking collectives: 631 us -> 0 us
  Pallas kernels: 0 us -> 78 us
  matrix products: 29 us -> 0 us
    reduce_scatter x2 -> x0, waiting for transfers between devices: 896 us -> none  [the longest x1 859 us: on_device(): lax.psum_scatter(hidden_terms, ('seq', 'tensor'), scatter_dimension=0, ti...]
    psum x1 -> x0, blocking collectives: 339 us -> none  [softmax_gradients(): lax.psum((jnp.sum(shifted, axis=1), local_target), ('seq', 'tensor'))]
    pmax x1 -> x0, blocking collectives: 292 us -> none  [softmax_gradients(): row_max = lax.pmax(jnp.max(logits, axis=1), ('seq', 'tensor'))]
    all_gather x2 -> x0, waiting for transfers between devices: 96.7 us -> none  [the longest x1 65.7 us: on_device(): window = lax.all_gather(hidden, 'seq', axis=0, tiled=True)]
    pallas_call x0 -> x1, Pallas kernels: none -> 78 us  [on_device(): pl.pallas_call(kernel, out_shape=tuple((pltpu.VMEM(*out) for out in outs)...]
    dot_general x3 -> x0, matrix products: 29 us -> none  [the longest x1 13.2 us: on_device(): jnp.einsum('vqj,jds->vdqs', derivative_pieces, coefficient_panels, prefer...]
  transfers between devices with their start and end apart: 4 -> 0, of which waited for: 4 -> 0; matrix products, arithmetic and copies ran while one was open for 1% -> 0% of each run, Pallas kernels for 0% -> 0%
where the time goes in v2:
time: 83.6 us; the launch traced here: 82.2 us
  Pallas kernels  78 us (93%)
  local copies, waits for them, and re-layouts  3.57 us (4%)
    pallas_call x1, Pallas kernels, on_device(): pl.pallas_call(kernel, out_shape=tuple((pltpu.VMEM(*out) for out in outs)...  78 us
    unnamed x3, local copies, waits for them, and re-layouts  3.57 us

profile of v2, /device:TPU:24, one launch (start us, length us, event | category | flops | bytes accessed | tf_op | source)
XLA Modules:
  0.0 82.2 jit_solution(77073858700191183)
XLA Ops:
  0.6 78.0 %head.1 = (bf16[32,336]{1,0:T(8,128)(2,1)S(1)}, bf16[1024,2688]{1,0:T(8,128)(2,1)S(1)}, f32[1,32]{1,0:T(1,128)S(1)}) custom-call(bf16[32,5376]{1,0:T(8,128)(2,1)} %hid.1, bf16[1024,2688]{1,0:T(8,128)(2,1)} %w.1, s32[4,128]{1,0:T(4,128)} %bitcast.5, s32[4,128]{1,0:T(4,128)} %bitcast.6, s32[4,128]{1,0:T(4,128)} %bitcast.7, s32[8]{0:T(128)} %cnt.1, f32[8]{0:T(128)} %sw.1), custom_call_target="tpu_custom_call" | custom-call | tf_op jit(solution)/shard_map/head/pallas_call | solution.py:331
  78.7 0.6 copy.13
  79.3 0.5 copy.15
  79.8 2.4 %copy.14 = bf16[1024,2688]{1,0:T(8,128)(2,1)} copy(bf16[1024,2688]{1,0:T(8,128)(2,1)S(1)} %get-tuple-element.10) | data formatting | bytes 11010048

commit v3 on v2

v3 whole, which is shorter than its diff:
```python
import functools

import jax
import jax.numpy as jnp
from jax import lax
from jax.experimental import pallas as pl
from jax.experimental.pallas import tpu as pltpu
from jax.sharding import PartitionSpec as P

MESH = pl.DeviceIdType.MESH
F32, BF16 = jnp.float32, jnp.bfloat16
V, D, HALF = 1024, 5376, 2688
WA = 1408
WB = HALF - WA
FW = 336
NN = (((1,), (0,)), ((), ()))
NT = (((1,), (1,)), ((), ()))


def device(x, y, z, c):
    return (c, x * 2 + y // 2, (y % 2) * 8 + z)


def aligned(index, unit):
    return pl.multiple_of(index * unit, unit)


def landed(ref, sem):
    pltpu.make_async_copy(ref, ref, sem).wait()


def merge(tiles):
    top = functools.reduce(jnp.maximum, [t[0:2] for t in tiles])
    total = sum(t[2:4] * jnp.exp(t[0:2] - top) for t in tiles)
    target = sum(t[4:6] for t in tiles)
    return [jnp.concatenate([v[0:1], v[1:2]], axis=1) for v in (top, total, target)]


def kernel(
    hid, w, tgt_in, strm_in, msk_in, cnt_in, sw_in,
    gh, gw, loss,
    tgt, strm, msk, cnt, sw, wv, hf, hs, lg, et, st_x, st_y, st_z, gt, g, p, lossbuf,
    fa, xa, ya_src, ya, fb, yb, xb_src, xb, fin, zs, zr,
    sem_far, sem_in, sem_w, sem_send, sem_own, sem_x, sem_c, sem_q, sem_p, sem_st, sem_g,
    sem_fa, sem_xa, sem_ya, sem_fb, sem_yb, sem_xb, sem_z,
):
    c, s, t = lax.axis_index("dp"), lax.axis_index("seq"), lax.axis_index("tensor")
    x, yh, yl, z = s // 2, s % 2, t // 8, t % 8
    y = yh * 2 + yl
    sib = device(x, y, z, 1 - c)
    xo = lambda o: (x + o) % 4
    yo = lambda o: (y + o) % 4
    zo = lambda o: (z + o) % 8
    cross = device(x, 3 - y, z, c)
    sends = []

    def send(src, dst, rsem, dev, unless=None):
        cp = pltpu.make_async_remote_copy(
            src_ref=src, dst_ref=dst, send_sem=sem_send.at[len(sends)], recv_sem=rsem,
            device_id=dev, device_id_type=MESH,
        )
        sends.append((cp, unless))
        if unless is None:
            cp.start()
        else:
            pl.when(jnp.logical_not(unless))(cp.start)

    half = z % 2

    def blk(h, bx, by, r0=0, n=32):
        return hf.at[h, pl.ds(pl.multiple_of((bx * 2 + by) * 32 + r0, 16), n), :]

    pairs = ((tgt_in, tgt), (strm_in, strm), (msk_in, msk), (cnt_in, cnt), (sw_in, sw))
    own = [pltpu.make_async_copy(a, b, sem_in.at[i]) for i, (a, b) in enumerate(pairs)]
    own += [
        pltpu.make_async_copy(hid.at[:, pl.ds(h * HALF, HALF)], blk(h, x, yh), sem_own.at[h])
        for h in range(2)
    ]
    for cp in own:
        cp.start()
    wcopy = pltpu.make_async_copy(w, wv.at[c], sem_w.at[0])
    wcopy.start()

    barrier = pltpu.get_barrier_semaphore()
    near_z = [device(x, y, zo(o), c) for o in (1, 7)]
    near_y = [device(x, yo(o), z, c) for o in (1, 3)]

    def tell(sem, peers):
        for peer in peers:
            pl.semaphore_signal(sem, inc=1, device_id=peer, device_id_type=MESH)

    tell(barrier, [sib] + [device(xo(o), y, z, c) for o in range(1, 4)] + near_y + near_z)
    pl.semaphore_wait(barrier, 8)
    tell(sem_far.at[0], near_y + near_z)

    def heard(i):
        pl.semaphore_wait(sem_far.at[i], 2 if i else 4)
        if i < 2:
            tell(sem_far.at[i + 1], near_z)

    partner = device(x, yh * 2 + 1 - yl, z, c)

    def z_send(ref, slot, r):
        send(ref, ref, sem_p.at[slot, r], device(x, y, zo(1 + 6 * r), c))

    def gather_start():
        mine = hid.at[:, pl.ds(aligned(half, HALF), HALF)]
        for o in (1, 3, 2):
            send(mine, blk(half, x, yh), sem_x.at[o - 1], device(xo(o), y, z, c))
        rows = pl.ds(aligned(1 - yl, 16), 16)
        part = hid.at[rows, pl.ds(aligned(half, HALF), HALF)]
        send(part, blk(half, x, yh, (1 - yl) * 16, 16), sem_c.at[0], cross)
        send(w, wv.at[c], sem_w.at[1], sib)

    def gather_x(o):
        landed(blk(half, xo(o), yh), sem_x.at[3 - o])
        ref = blk(half, xo(o), yh) if o == 2 else blk(half, xo(o), yh, (1 - yl) * 16, 16)
        send(ref, ref, sem_c.at[o], cross)
        for r in range(2):
            z_send(blk(half, xo(o), yh, r * 16, 16), o, r)

    def gather_y(o):
        if o == 2:
            landed(blk(half, xo(o), 1 - yh), sem_c.at[o])
            for r in range(2):
                z_send(blk(half, xo(o), 1 - yh, r * 16, 16), 4 + o, r)
        else:
            ref = blk(half, xo(o), 1 - yh, yl * 16, 16)
            landed(ref, sem_c.at[o])
            send(ref, ref, sem_q.at[o], partner)
            z_send(ref, 4 + o, yl)

    def gather_partner(o):
        ref = blk(half, xo(o), 1 - yh, (1 - yl) * 16, 16)
        landed(ref, sem_q.at[o])
        z_send(ref, 4 + o, 1 - yl)

    def gather_end():
        for r in range(2):
            for o in range(1, 4):
                landed(blk(1 - half, xo(o), yh, r * 16, 16), sem_p.at[o, r])
            for o in range(4):
                landed(blk(1 - half, xo(o), 1 - yh, r * 16, 16), sem_p.at[4 + o, r])

    def gather_local():
        for cp in own:
            cp.wait()
        wcopy.wait()
        landed(wv.at[1 - c], sem_w.at[1])

    def logits(h, add=False):
        def tile(i, _):
            rows = pl.ds(aligned(i, 512), 512)
            out = lax.dot_general(wv[h, rows, :], hf[h], NT, preferred_element_type=F32)
            lg[rows, :] = lg[rows, :] + out if add else out
            return 0

        lax.fori_loop(0, 2, tile, 0)

    def row(ref):
        return jnp.concatenate([ref[pl.ds(2 * c, 1), :], ref[pl.ds(2 * c + 1, 1), :]], axis=1)

    def vocab_hit(i):
        ids = (s * 16 + t) * V + i * 256 + lax.broadcasted_iota(jnp.int32, (256, 256), 0)
        return ids == row(tgt)

    def local_stats():
        def highest(i, top):
            return jnp.maximum(top, jnp.max(lg[pl.ds(aligned(i, 256), 256), :], axis=0, keepdims=True))

        top = lax.fori_loop(0, 4, highest, jnp.full((1, 256), -jnp.inf, F32))

        def expo(i, carry):
            total, target = carry
            rows = pl.ds(aligned(i, 256), 256)
            logit = lg[rows, :]
            e = jnp.exp(logit - top)
            lg[rows, :] = e
            target += jnp.sum(jnp.where(vocab_hit(i), logit, 0.0), axis=0, keepdims=True)
            return total + jnp.sum(e, axis=0, keepdims=True), target

        zero = jnp.zeros((1, 256), F32)
        total, target = lax.fori_loop(0, 4, expo, (zero, zero))
        return top, total, target

    def exchange(buf, vals, n, base, dev, meanwhile=None):
        rows = [v[:, i * 128:i * 128 + 128] for v in vals for i in range(2)]
        buf[0] = jnp.concatenate([*rows, jnp.zeros((2, 128), F32)], axis=0)
        for o in sorted(range(1, n), key=lambda o: -min(o, n - o)):
            send(buf.at[0], buf.at[o], sem_st.at[base + o], dev(o))
        if meanwhile is not None:
            meanwhile()
        for o in range(1, n):
            landed(buf.at[o], sem_st.at[base + o])
        return merge([buf[o] for o in range(n)])

    def turn():
        def tile(i, _):
            rows = pl.ds(aligned(i, 256), 256)
            et[:, rows] = lg[rows, :].T
            return 0

        lax.fori_loop(0, 4, tile, 0)

    def grads():
        vals = local_stats()
        top0 = vals[0]
        vals = exchange(st_x, vals, 4, 0, lambda o: device(xo(o), y, z, c), turn)
        vals = exchange(st_y, vals, 4, 4, lambda o: device(x, yo(o), z, c))
        fraction = jnp.zeros((1, 256), F32)
        for i in range(8):
            weight = jnp.full((1, 256), sw[i], F32)
            count = jnp.full((1, 256), cnt[i], jnp.int32).astype(F32)
            fraction = jnp.where(row(strm) == i, weight / count, fraction)
        mask = row(msk).astype(F32)
        scale = mask * fraction
        top, total, target = exchange(st_z, vals, 8, 8, lambda o: device(x, y, zo(o), c))
        norm = jnp.exp(top0 - top) / total
        stack = [norm, scale, row(tgt).astype(F32), jnp.zeros((5, 256), F32)]
        columns = jnp.concatenate(stack, axis=0).T
        norm_c, scale_c, target_c = columns[:, 0:1], columns[:, 1:2], columns[:, 2:3]
        first_id = ((s * 16 + t) * V).astype(F32)

        def tile(i, _):
            cols = pl.ds(aligned(i, 256), 256)
            place = i * 256 + lax.broadcasted_iota(jnp.int32, (256, 256), 1)
            hit = jnp.where(place.astype(F32) + first_id == target_c, 1.0, 0.0)
            g[:, cols] = (scale_c * (et[:, cols] * norm_c - hit)).astype(BF16)
            return 0

        lax.fori_loop(0, 4, tile, 0)
        row_loss = mask * (top + jnp.log(total) - target)
        for h in range(2):
            lossbuf[h] = jnp.broadcast_to(row_loss[:, h * 128:h * 128 + 128], (8, 128))
        return norm, scale

    def grads_turned(norm, scale):
        def tile(i, _):
            rows = pl.ds(aligned(i, 256), 256)
            hit = jnp.where(vocab_hit(i), 1.0, 0.0)
            gt[c, rows, :] = (scale * (lg[rows, :] * norm - hit)).astype(BF16)
            return 0

        lax.fori_loop(0, 4, tile, 0)
        send(gt.at[c], gt.at[c], sem_g.at[0], sib)

    ca, cb = pl.ds(0, WA), pl.ds(WA, WB)

    def products(h, lo, n):
        def columns(cols, width):
            out = lax.dot_general(g[...], wv[h, :, cols], NN, preferred_element_type=F32)
            p[h, :, :, :, cols] = out.astype(BF16).reshape(4, 2, 32, width)

        def tile(i, _):
            columns(pl.ds(pl.multiple_of(lo + i * 256, 128), 256), 256)
            return 0

        lax.fori_loop(0, n // 256, tile, 0)
        if n % 256:
            columns(pl.ds(lo + n // 256 * 256, n % 256), n % 256)

    def a_first(h):
        products(h, 0, WA)
        for j, o in enumerate((1, 3)):
            dev = device(xo(o), y, z, c)
            send(p.at[h, xo(2), j, :, ca], fa.at[h, j], sem_fa.at[h, j], dev)
            send(p.at[h, xo(o), 1 - j, :, ca], xa.at[h, j, 1 - j], sem_xa.at[h, j, 1 - j], dev)

    def a_mid(h):
        for j, o in enumerate((1, 3)):
            landed(fa.at[h, j], sem_fa.at[h, j])
            both = p[h, xo(o), j, :, 0:WA].astype(F32) + fa[h, j].astype(F32)
            p[h, xo(o), j, :, 0:WA] = both.astype(BF16)
            send(p.at[h, xo(o), j, :, ca], xa.at[h, j, j], sem_xa.at[h, j, j],
                 device(xo(o), y, z, c))

    def a_second(h):
        for k in range(2):
            total = p[h, x, k, :, 0:WA].astype(F32)
            for j in range(2):
                landed(xa.at[h, j, k], sem_xa.at[h, j, k])
                total += xa[h, j, k].astype(F32)
            ya_src[h, k] = total.astype(BF16)
            there = 2 * k + h
            send(ya_src.at[h, k], ya.at[y], sem_ya.at[y], device(x, there, z, c), there == y)

    def piece(there, j):
        return p.at[there % 2, pl.ds(2 * j, 2), there // 2, :, cb]

    def b_first():
        products(yl, WA, WB)
        for j, o in enumerate((1, 3)):
            send(piece(yo(2), j), fb.at[j], sem_fb.at[j], device(x, yo(o), z, c))
        products(1 - yl, WA, WB)
        for j, o in enumerate((1, 3)):
            there = yo(o)
            send(piece(there, 1 - j), yb.at[j, 1 - j], sem_yb.at[j, 1 - j],
                 device(x, there, z, c))

    def b_mid():
        for j, o in enumerate((1, 3)):
            there = yo(o)
            landed(fb.at[j], sem_fb.at[j])
            ref = piece(there, j)
            ref[...] = (ref[...].astype(F32) + fb[j].astype(F32)).astype(BF16)
            send(ref, yb.at[j, j], sem_yb.at[j, j], device(x, there, z, c))

    def b_second():
        for k in range(4):
            total = p[yl, k, yh, :, WA:HALF].astype(F32)
            for j in range(2):
                if k % 2 == 0:
                    landed(yb.at[j, k // 2], sem_yb.at[j, k // 2])
                total += yb[j, k // 2, k % 2].astype(F32)
            xb_src[k] = total.astype(BF16)
        for o in (2, 1, 3):
            send(xb_src.at[xo(o)], xb.at[o - 1], sem_xb.at[o - 1], device(xo(o), y, z, c))

    def last():
        total = ya_src[yl, yh].astype(F32)
        for o in range(1, 4):
            landed(ya.at[yo(o)], sem_ya.at[yo(o)])
            total += ya[yo(o)].astype(F32)
        fin[:, 0:WA] = total
        total = xb_src[x].astype(F32)
        for o in range(3):
            landed(xb.at[o], sem_xb.at[o])
            total += xb[o].astype(F32)
        fin[:, WA:HALF] = total
        for i in range(8):
            lo = i * FW // 128 * 128
            wide = min(512, HALF - lo)
            window = fin[:, lo:lo + wide]
            shift = i * FW - lo
            if shift:
                window = pltpu.roll(window, wide - shift, 1)
            zs[i] = window[:, :384].astype(BF16)
        for o in (4, 3, 5, 2, 6, 1, 7):
            send(zs.at[zo(o)], zr.at[o - 1], sem_z.at[o - 1], device(x, y, zo(o), c))

    def end():
        total = zs[z].astype(F32)
        for o in range(7):
            landed(zr.at[o], sem_z.at[o])
            total += zr[o].astype(F32)
        gh[...] = total[:, :FW].astype(BF16)
        row_loss = lossbuf[x // 2]
        row_loss = pltpu.roll(row_loss, (128 - (x % 2) * 64 - yh * 32) % 128, 1)
        loss[...] = row_loss[0:1, 0:32]

    def head_tile(cols):
        out = lax.dot_general(gt[c], hf[c, :, cols], NN, preferred_element_type=F32)
        out += lax.dot_general(gt[1 - c], hs[:, cols], NN, preferred_element_type=F32)
        gw[:, cols] = out.astype(BF16)

    def head_grad(lo, hi):
        if lo == 0:
            landed(gt.at[1 - c], sem_g.at[0])
            landed(hs, sem_g.at[1])

        def tile(i, _):
            head_tile(pl.ds(aligned(i, 256), 256))
            return 0

        lax.fori_loop(lo, hi, tile, 0)
        if hi == 10:
            head_tile(pl.ds(2560, 128))

    gather_start()
    gather_x(1)
    heard(0)
    gather_x(3)
    heard(1)
    gather_y(0)
    gather_partner(0)
    gather_x(2)
    gather_y(1)
    gather_y(3)
    gather_partner(1)
    gather_partner(3)
    gather_y(2)
    heard(2)
    gather_local()
    logits(half)
    gather_end()
    logits(1 - half, True)
    send(hf.at[1 - c], hs, sem_g.at[1], sib)
    norm, scale = grads()
    a_first(0)
    b_first()
    a_first(1)
    a_mid(0)
    grads_turned(norm, scale)
    b_mid()
    a_mid(1)
    head_grad(0, 6)
    a_second(0)
    head_grad(6, 10)
    a_second(1)
    b_second()
    last()
    end()
    for cp, unless in sends:
        if unless is None:
            cp.wait_send()
        else:
            pl.when(jnp.logical_not(unless))(cp.wait_send)


def on_device(hidden, weight, targets, streams, loss_token_mask, counts, stream_weight):
    vm = pl.BlockSpec(memory_space=pltpu.VMEM)
    hbm = pl.BlockSpec(memory_space=pl.ANY)
    dma = pltpu.SemaphoreType.DMA
    rows = lambda a: a.reshape(4, 128)
    outs = (((32, FW), BF16), ((V, HALF), BF16), ((1, 32), F32))
    gh, gw, loss = pl.pallas_call(
        kernel,
        out_shape=tuple(pltpu.VMEM(*out) for out in outs),
        in_specs=[hbm] * 7,
        out_specs=(vm, vm, vm),
        scratch_shapes=[
            pltpu.VMEM((4, 128), jnp.int32),
            pltpu.VMEM((4, 128), jnp.int32),
            pltpu.VMEM((4, 128), jnp.int32),
            pltpu.SMEM((8,), jnp.int32),
            pltpu.SMEM((8,), F32),
            pltpu.VMEM((2, V, HALF), BF16),
            pltpu.VMEM((2, 256, HALF), BF16),
            pltpu.VMEM((256, HALF), BF16),
            pltpu.VMEM((V, 256), F32),
            pltpu.VMEM((256, V), F32),
            pltpu.VMEM((4, 8, 128), F32),
            pltpu.VMEM((4, 8, 128), F32),
            pltpu.VMEM((8, 8, 128), F32),
            pltpu.VMEM((2, V, 256), BF16),
            pltpu.VMEM((256, V), BF16),
            pltpu.VMEM((2, 4, 2, 32, HALF), BF16),
            pltpu.VMEM((2, 8, 128), F32),
            pltpu.VMEM((2, 2, 32, WA), BF16),
            pltpu.VMEM((2, 2, 2, 32, WA), BF16),
            pltpu.VMEM((2, 2, 32, WA), BF16),
            pltpu.VMEM((4, 32, WA), BF16),
            pltpu.VMEM((2, 2, 32, WB), BF16),
            pltpu.VMEM((2, 2, 2, 32, WB), BF16),
            pltpu.VMEM((4, 32, WB), BF16),
            pltpu.VMEM((3, 32, WB), BF16),
            pltpu.VMEM((32, HALF), F32),
            pltpu.VMEM((8, 32, 384), BF16),
            pltpu.VMEM((7, 32, 384), BF16),
            pltpu.SemaphoreType.REGULAR((3,)),
            dma((5,)), dma((2,)), dma((128,)), dma((2,)), dma((3,)), dma((4,)), dma((4,)), dma((8, 2)), dma((16,)),
            dma((2,)),
            dma((2, 2)), dma((2, 2, 2)), dma((4,)), dma((2,)), dma((2, 2)), dma((3,)), dma((7,)),
        ],
        compiler_params=pltpu.CompilerParams(
            collective_id=0, has_side_effects=True, vmem_limit_bytes=56 << 20
        ),
        name="head",
    )(hidden, weight, rows(targets), rows(streams), rows(loss_token_mask), counts, stream_weight)
    return gh, gw, loss.reshape(32)


def solution(mesh):
    in_specs = (P(("dp", "seq"), None), P(("seq", "tensor"), "dp"), P(), P(), P(), P(), P())
    out_specs = (P(("dp", "seq"), "tensor"), P(("seq", "tensor"), "dp"), P(("dp", "seq")))
    return jax.shard_map(
        on_device, mesh=mesh, in_specs=in_specs, out_specs=out_specs, check_vma=False
    )
```

time: 83.6 us -> 77.8 us (0.931)
  Pallas kernels: 78 us -> 72.7 us
    pallas_call x1, Pallas kernels: 78 us -> 72.7 us  [on_device(): pl.pallas_call(kernel, out_shape=tuple((pltpu.VMEM(*out) for out in outs)...]
where the time goes in v3:
time: 77.8 us; the launch traced here: 76.9 us
  Pallas kernels  72.7 us (93%)
  local copies, waits for them, and re-layouts  3.57 us (5%)
    pallas_call x1, Pallas kernels, on_device(): pl.pallas_call(kernel, out_shape=tuple((pltpu.VMEM(*out) for out in outs)...  72.7 us
    unnamed x3, local copies, waits for them, and re-layouts  3.57 us

profile of v3, /device:TPU:24, one launch (start us, length us, event | category | flops | bytes accessed | tf_op | source)
XLA Modules:
  0.0 76.9 jit_solution(3216738321564767910)
XLA Ops:
  0.6 72.7 %head.1 = (bf16[32,336]{1,0:T(8,128)(2,1)S(1)}, bf16[1024,2688]{1,0:T(8,128)(2,1)S(1)}, f32[1,32]{1,0:T(1,128)S(1)}) custom-call(bf16[32,5376]{1,0:T(8,128)(2,1)} %hid.1, bf16[1024,2688]{1,0:T(8,128)(2,1)} %w.1, s32[4,128]{1,0:T(4,128)} %bitcast.5, s32[4,128]{1,0:T(4,128)} %bitcast.6, s32[4,128]{1,0:T(4,128)} %bitcast.7, s32[8]{0:T(128)} %cnt_in.1, f32[8]{0:T(128)} %sw_in.1), custom_call_target="tpu_custom_call" | custom-call | tf_op jit(solution)/shard_map/head/pallas_call | solution.py:416
  73.4 0.6 copy.13
  74.0 0.5 copy.15
  74.5 2.4 %copy.14 = bf16[1024,2688]{1,0:T(8,128)(2,1)} copy(bf16[1024,2688]{1,0:T(8,128)(2,1)S(1)} %get-tuple-element.10) | data formatting | bytes 11010048

commit v4 on v3

--- a/solution.py
+++ b/solution.py
@@ -389,11 +389,12 @@
     a_first(0)
     b_first()
     a_first(1)
+    grads_turned(norm, scale)
     a_mid(0)
-    grads_turned(norm, scale)
     b_mid()
+    head_grad(0, 2)
     a_mid(1)
-    head_grad(0, 6)
+    head_grad(2, 6)
     a_second(0)
     head_grad(6, 10)
     a_second(1)

time: 77.8 us -> 77.5 us (level); the launches traced: 76.9 us -> 77.4 us
  no operation moved by 1% of the time
where the time goes in v4:
time: 77.5 us; the launch traced here: 77.4 us
  Pallas kernels  73.2 us (94%)
  local copies, waits for them, and re-layouts  3.57 us (5%)
    pallas_call x1, Pallas kernels, on_device(): pl.pallas_call(kernel, out_shape=tuple((pltpu.VMEM(*out) for out in outs)...  73.2 us
    unnamed x3, local copies, waits for them, and re-layouts  3.57 us

profile of v4, /device:TPU:24, one launch (start us, length us, event | category | flops | bytes accessed | tf_op | source)
XLA Modules:
  0.0 77.4 jit_solution(3335304035541541638)
XLA Ops:
  0.6 73.2 %head.1 = (bf16[32,336]{1,0:T(8,128)(2,1)S(1)}, bf16[1024,2688]{1,0:T(8,128)(2,1)S(1)}, f32[1,32]{1,0:T(1,128)S(1)}) custom-call(bf16[32,5376]{1,0:T(8,128)(2,1)} %hid.1, bf16[1024,2688]{1,0:T(8,128)(2,1)} %w.1, s32[4,128]{1,0:T(4,128)} %bitcast.5, s32[4,128]{1,0:T(4,128)} %bitcast.6, s32[4,128]{1,0:T(4,128)} %bitcast.7, s32[8]{0:T(128)} %cnt_in.1, f32[8]{0:T(128)} %sw_in.1), custom_call_target="tpu_custom_call" | custom-call | tf_op jit(solution)/shard_map/head/pallas_call | solution.py:417
  73.9 0.6 copy.13
  74.5 0.5 copy.15
  75.0 2.4 %copy.14 = bf16[1024,2688]{1,0:T(8,128)(2,1)} copy(bf16[1024,2688]{1,0:T(8,128)(2,1)S(1)} %get-tuple-element.10) | data formatting | bytes 11010048
